TPU v7x, 32 devices: a whole 2x2x4 slice. The times are simulated.
32 devices in a mesh: grp: 4 (over z), nbr: 8 (over y, x, core).
Axes of the slice: x: 2, y: 2, z: 4, core: 2. Of those that a mesh axis runs over, the one named last changes fastest.
Arguments:
- fine_coef: bfloat16 [256, 1024], P(('grp', 'nbr')), may hold values from -6 to 6
- fine_live: int32 [32], P(('grp', 'nbr')), may hold values from 2 to 8, as said below
- fine_parent: int32 [256], P(('grp', 'nbr')), may hold values from 0 to 31, as said below
- up_transfer: bfloat16 [256, 1024], P(('grp', 'nbr')), may hold values from -1 to 1
- fine_list: int32 [256, 96], P(('grp', 'nbr')), may hold values from 0 to 255, as said below
- fine_nblk: int32 [256], P(('grp', 'nbr')), may hold values from 24 to 96, as said below
- fine_blocks: bfloat16 [256, 96, 1024], P(('grp', 'nbr')), may hold values from -1 to 1
- fine_scale: float32 [256, 96], P(('grp', 'nbr')), may hold values from 0.03 to 0.3
- coarse_list: int32 [32, 96], P(('grp', 'nbr')), may hold values from 0 to 31
- coarse_nblk: int32 [32], P(('grp', 'nbr')), may hold values from 24 to 96, as said below
- coarse_blocks: bfloat16 [32, 96, 1024], P(('grp', 'nbr')), may hold values from -1 to 1
- coarse_scale: float32 [32, 96], P(('grp', 'nbr')), may hold values from 0.01 to 0.1
- down_transfer: bfloat16 [256, 1024], P(('grp', 'nbr')), may hold values from -1 to 1
Outputs:
- fine_local: bfloat16 [256, 1024], P(('grp', 'nbr'))
Inputs may be any that keep to these rules, and one draw needn't show every extreme that they name: `fine_live`: one owner in every draw holds all 8 slots. `fine_parent`: the parent of a fine slot lies in the same subtree group: slots g * 64 to (g + 1) * 64 - 1 have parents g * 8 to (g + 1) * 8 - 1. `fine_list`: every entry of a fine box's list is a live slot of the box's own subtree group. `fine_nblk`: some live box uses all 96 entries in every draw. `coarse_nblk`: some box uses all 96 entries in every draw.
All inputs are finite; a program needn't handle non-finite values.
Results may differ from a plain program's by a relative error of at most 0.0044.
Values may be sent and summed in bfloat16 or wider, within the bound.
A program may use at most 64 MiB of HBM per device.

v0:
```python
import jax
import jax.numpy as jnp
from jax import lax
from jax.sharding import PartitionSpec as P

K = 32
R = 32


def couple(blocks, scale, count, picked):
    slots = blocks.shape[0]
    width = blocks.shape[1]
    prod = jnp.einsum(
        "tjik,tjkr->tjir",
        blocks.reshape(slots, width, K, K),
        picked.reshape(slots, width, K, R),
        preferred_element_type=jnp.float32,
    )
    used = jnp.arange(width)[None, :] < count[:, None]
    weight = jnp.where(used, scale, jnp.float32(0.0))
    return jnp.sum(prod * weight[:, :, None, None], axis=1)


def body(
    fine_coef,
    fine_live,
    fine_parent,
    up_transfer,
    fine_list,
    fine_nblk,
    fine_blocks,
    fine_scale,
    coarse_list,
    coarse_nblk,
    coarse_blocks,
    coarse_scale,
    down_transfer,
):
    slots = fine_coef.shape[0]
    coarse_slots = coarse_blocks.shape[0]
    members = lax.axis_size("nbr")
    group = lax.axis_index("grp")
    live = jnp.arange(slots) < fine_live[0]
    source = jnp.where(live[:, None], fine_coef, jnp.zeros_like(fine_coef))
    group_coarse = coarse_slots * members
    local_parent = fine_parent - group * group_coarse
    lifted = jnp.einsum(
        "bij,bjr->bir",
        up_transfer.reshape(slots, K, K),
        source.reshape(slots, K, R),
        preferred_element_type=jnp.float32,
    ).reshape(slots, K * R)
    onehot = (local_parent[:, None] == jnp.arange(group_coarse)[None, :]).astype(jnp.float32)
    summed = lax.psum(
        jnp.dot(
            onehot.T, lifted, precision=lax.Precision.HIGHEST, preferred_element_type=jnp.float32
        ),
        "nbr",
    )
    everything = lax.all_gather(summed.astype(jnp.bfloat16), "grp", axis=0, tiled=True)
    group_sources = lax.all_gather(source, "nbr", axis=0, tiled=True)
    picked_coarse = everything[coarse_list]
    coarse_local = couple(coarse_blocks, coarse_scale, coarse_nblk, picked_coarse)
    coarse_local = coarse_local.reshape(coarse_slots, K * R).astype(jnp.bfloat16)
    local_source = fine_list - group * (slots * members)
    near = couple(fine_blocks, fine_scale, fine_nblk, group_sources[local_source])
    group_local = lax.all_gather(coarse_local, "nbr", axis=0, tiled=True)
    parent_rows = group_local[local_parent]
    down = jnp.einsum(
        "bij,bjr->bir",
        down_transfer.reshape(slots, K, K),
        parent_rows.reshape(slots, K, R),
        preferred_element_type=jnp.float32,
    )
    total = jnp.where(live[:, None, None], near + down, jnp.float32(0.0))
    return total.reshape(slots, K * R).astype(jnp.bfloat16)


def solution(mesh):
    placed = (
        P(("grp", "nbr"), None),
        P(("grp", "nbr")),
        P(("grp", "nbr")),
        P(("grp", "nbr"), None),
        P(("grp", "nbr"), None),
        P(("grp", "nbr")),
        P(("grp", "nbr"), None, None),
        P(("grp", "nbr"), None),
        P(("grp", "nbr"), None),
        P(("grp", "nbr")),
        P(("grp", "nbr"), None, None),
        P(("grp", "nbr"), None),
        P(("grp", "nbr"), None),
    )
    return jax.shard_map(
        body, mesh=mesh, in_specs=placed, out_specs=P(("grp", "nbr"), None), check_vma=False
    )
```

profile of v0, /device:TPU:0, one launch (start us, length us, event | category | flops | bytes accessed | tf_op | source)
XLA Modules:
  0.0 99.4 jit_solution(2779841631882370184)
XLA Ops:
  0.0 0.8 fusion.3
  1.4 0.8 broadcast_select_fusion
  2.2 10.7 %all_gather.9 = bf16[64,1024]{1,0:T(8,128)(2,1)S(1)} all-gather(bf16[8,1024]{1,0:T(8,128)(2,1)S(1)} %broadcast_select_fusion), channel_id=1, replica_groups=mesh['grp'=4,'nbr'=8] {'nbr'}, dimensions={0}, use_global_device_ids=true | all-gather | bytes 147456 | tf_op jit(solution)/shard_map/all_gather | solution.py:61
  12.9 0.7 compare_select_fusion
  13.6 0.1 reshape.87
  13.7 2.8 %gather_fusion = bf16[768,1024]{1,0:T(8,128)(2,1)S(1)} fusion(bf16[64,1024]{1,0:T(8,128)(2,1)S(1)} %all_gather.9, s32[1024]{0:T(1024)S(1)} %pad_clamp_fusion.2), kind=kCustom, calls=%fused_computation | custom fusion | bytes 3148800 | tf_op jit(solution)/shard_map/gather | solution.py:66
  16.5 1.6 %copy.42 = bf16[768,1024]{0,1:T(8,128)(2,1)} copy(bf16[768,1024]{1,0:T(8,128)(2,1)S(1)} %gather_fusion) | data formatting | bytes 3145728 | tf_op jit(solution)/shard_map/gather | solution.py:66
  18.1 3.7 %reshape.76 = bf16[8,96,32,32]{1,0,3,2:T(8,128)(2,1)S(1)} reshape(bf16[768,1024]{0,1:T(8,128)(2,1)} %copy.42) | data formatting | bytes 3145728 | tf_op jit(solution)/shard_map/reshape | solution.py:16
  21.8 5.7 %copy.44 = bf16[8,96,32,32]{2,3,1,0:T(8,128)(2,1)} copy(bf16[8,96,32,32]{1,0,3,2:T(8,128)(2,1)S(1)} %reshape.76) | data formatting | bytes 3145728 | tf_op jit(solution)/shard_map/reshape | solution.py:16
  27.5 2.9 %copy.43 = bf16[8,96,1024]{1,2,0:T(8,128)(2,1)S(1)} copy(bf16[8,96,1024]{2,1,0:T(8,128)(2,1)} %param.19) | data formatting | bytes 3145728 | tf_op args[6]
  30.4 6.6 %copy.45 = bf16[8,96,32,32]{3,2,1,0:T(8,128)(2,1)} copy(bf16[8,96,32,32]{1,3,2,0:T(8,128)(2,1)S(1)} %bitcast.32) | data formatting | bytes 3145728 | tf_op jit(solution)/shard_map/reshape | solution.py:15
  37.1 0.0 copy-start.1
  37.1 0.0 copy-start.3
  37.1 0.0 copy-start.4
  37.1 0.0 copy-start
  37.1 0.0 copy-start.5
  37.1 8.1 %multiply_reduce_fusion = f32[8,32,32]{2,1,0:T(8,128)S(1)} fusion(f32[8,96]{1,0:T(8,128)S(1)} %fusion.3, bf16[8,96,32,32]{2,3,1,0:T(8,128)(2,1)} %copy.44, bf16[8,96,32,32]{3,2,1,0:T(8,128)(2,1)} %copy.45), kind=kOutput, calls=%fused_computation.3 | convolution fusion | flops 51896320 | bytes 3181568 | tf_op jit(solution)/shard_map/tjik,tjkr->tjir/dot_general | solution.py:13
  45.2 0.0 copy-start.2
  45.2 0.1 reshape.78
  45.3 0.0 copy-done.1
  45.3 0.1 reshape.79
  45.4 0.2 convolution_bitcast_fusion
  45.6 0.1 copy.47
  45.7 0.1 reshape.80
  45.8 0.0 copy-done.3
  45.9 0.3 fusion.4
  46.1 23.6 %psum.7 = bf16[8,1024]{1,0:T(8,128)(2,1)S(1)} all-reduce(f32[8,1024]{1,0:T(8,128)S(1)} %fusion.4), channel_id=1, replica_groups=mesh['grp'=4,'nbr'=8] {'nbr'}, use_global_device_ids=true, to_apply=%region_1.2 | all-reduce | flops 8192 | bytes 49152 | tf_op jit(solution)/shard_map/psum | solution.py:54
  69.7 13.6 %all_gather.10 = bf16[32,1024]{1,0:T(8,128)(2,1)S(1)} all-gather(bf16[8,1024]{1,0:T(8,128)(2,1)S(1)} %psum.7), channel_id=1, replica_groups=mesh['grp'=4,'nbr'=8] {'grp'}, dimensions={0}, use_global_device_ids=true | all-gather | bytes 81920 | tf_op jit(solution)/shard_map/all_gather | solution.py:60
  83.3 0.0 copy-done.4
  83.3 0.8 gather_fusion.1
  84.1 0.2 copy.48
  84.3 1.3 %copy.50 = bf16[96,32,32]{1,2,0:T(8,128)(2,1)S(1)} copy(bf16[96,32,32]{0,2,1:T(8,128)(2,1)S(1)} %bitcast.34) | data formatting | bytes 393216 | tf_op jit(solution)/shard_map/reshape.1
  85.6 0.0 copy-done
  85.6 0.2 copy.49
  85.8 1.2 %copy.51 = bf16[96,32,32]{2,1,0:T(8,128)(2,1)S(1)} copy(bf16[96,32,32]{0,2,1:T(8,128)(2,1)S(1)} %bitcast.35) | data formatting | bytes 393216 | tf_op jit(solution)/shard_map/reshape
  87.7 0.0 copy-done.5
  87.7 0.5 multiply_reduce_fusion.1
  88.2 0.1 copy.52
  88.3 0.1 reshape.115
  88.4 9.1 %all-gather = bf16[8,1,1024]{2,1,0:T(2,128)(2,1)S(1)} all-gather(bf16[1,1,1024]{2,1,0:T(2,128)(2,1)S(1)} %reshape.115), channel_id=1, replica_groups=mesh['grp'=4,'nbr'=8] {'nbr'}, dimensions={0}, use_global_device_ids=true | all-gather | bytes 18432 | tf_op jit(solution)/shard_map/all_gather | solution.py:67
  97.5 0.6 gather_fusion.2
  98.1 0.1 reshape.83
  98.2 0.0 copy-done.2
  98.2 0.1 reshape.84
  98.3 0.2 fusion.2
  98.5 0.1 copy.54
  98.6 0.7 convert_element_type.36
  (8 shorter events, 0.1 us)
Async XLA Ops:
  37.1 8.2 %copy-start.1 = (bf16[8,1024]{1,0:T(8,128)(2,1)S(1)}, bf16[8,1024]{1,0:T(8,128)(2,1)}, u32[]{:S(2)}) copy-start(bf16[8,1024]{1,0:T(8,128)(2,1)} %param.16) | copy-start | bytes 49156
  37.1 8.8 %copy-start.3 = (s32[8]{0:T(128)S(1)}, s32[8]{0:T(128)}, u32[]{:S(2)}) copy-start(s32[8]{0:T(128)} %param.15) | copy-start | bytes 100
  37.1 46.3 %copy-start.4 = (s32[1,96]{1,0:T(1,128)S(1)}, s32[1,96]{1,0:T(1,128)}, u32[]{:S(2)}) copy-start(s32[1,96]{1,0:T(1,128)} %param.21) | copy-start | bytes 1156
  37.1 48.5 %copy-start = (bf16[1,96,1024]{2,1,0:T(8,128)(2,1)S(1)}, bf16[1,96,1024]{2,1,0:T(8,128)(2,1)}, u32[]{:S(2)}) copy-start(bf16[1,96,1024]{2,1,0:T(8,128)(2,1)} %param.23) | copy-start | bytes 589828
  37.1 50.6 %copy-start.5 = (f32[1,96]{1,0:T(1,128)S(1)}, f32[1,96]{1,0:T(1,128)}, u32[]{:S(2)}) copy-start(f32[1,96]{1,0:T(1,128)} %param.24) | copy-start | bytes 1156
  45.2 53.0 %copy-start.2 = (bf16[8,1024]{1,0:T(8,128)(2,1)S(1)}, bf16[8,1024]{1,0:T(8,128)(2,1)}, u32[]{:S(2)}) copy-start(bf16[8,1024]{1,0:T(8,128)(2,1)} %param.25) | copy-start | bytes 49156
where the time goes:
time: 99.8 us; the launch traced here: 99.4 us
  blocking collectives  56.9 us (57%)
  local copies, waits for them, and re-layouts  29.4 us (29%)
  matrix products  9.28 us (9%)
  other arithmetic  2.28 us (2%)
  between operations  1.52 us (2%)
    psum x1, blocking collectives, body(): lax.psum(jnp.dot(onehot.T, lifted, precision=lax.Precision.HIGHEST, prefe...  23.6 us
    all_gather x1, blocking collectives, body(): lax.all_gather(summed.astype(jnp.bfloat16), 'grp', axis=0, tiled=True)  13.6 us
    all_gather x1, blocking collectives, body(): group_sources = lax.all_gather(source, 'nbr', axis=0, tiled=True)  10.7 us
    reshape x2, local copies, waits for them, and re-layouts, couple(): picked.reshape(slots, width, K, R)  9.44 us
    all_gather x1, blocking collectives, body(): group_local = lax.all_gather(coarse_local, 'nbr', axis=0, tiled=True)  9.05 us
    dot_general x2, matrix products, couple(): jnp.einsum('tjik,tjkr->tjir', blocks.reshape(slots, width, K, K), picked....  8.59 us
    reshape x1, local copies, waits for them, and re-layouts, couple(): blocks.reshape(slots, width, K, K)  6.62 us
    gather x2, local copies, waits for them, and re-layouts, body(): group_sources[local_source]  4.4 us

commit v1 on v0

--- a/solution.py
+++ b/solution.py
@@ -57,7 +57,17 @@
         ),
         "nbr",
     )
-    everything = lax.all_gather(summed.astype(jnp.bfloat16), "grp", axis=0, tiled=True)
+    x = summed.astype(jnp.bfloat16)
+    ways = lax.axis_size("grp")
+    up = [(d, (d + 1) % ways) for d in range(ways)]
+    down_2 = [(d, (d - 1) % ways) for d in range(ways)]
+    earlier, later = ([x], [x])
+    for _ in range(ways // 2):
+        earlier.append(lax.ppermute(earlier[-1], "grp", up))
+    for _ in range((ways - 1) // 2):
+        later.append(lax.ppermute(later[-1], "grp", down_2))
+    line = jnp.concatenate([*earlier[::-1], *later[1:]], axis=0)
+    everything = jnp.roll(line, (lax.axis_index("grp") - ways // 2) * x.shape[0], axis=0)
     group_sources = lax.all_gather(source, "nbr", axis=0, tiled=True)
     picked_coarse = everything[coarse_list]
     coarse_local = couple(coarse_blocks, coarse_scale, coarse_nblk, picked_coarse)

time: 99.8 us -> 94.5 us (0.947)
  blocking collectives: 56.9 us -> 42.8 us
  starting transfers between devices: 0 us -> 4.06 us
  waiting for transfers between devices: 0 us -> 3.94 us
    all_gather x1 -> x0, blocking collectives: 13.6 us -> none  [body(): lax.all_gather(summed.astype(jnp.bfloat16), 'grp', axis=0, tiled=True)]
    ppermute x0 -> x3, starting transfers between devices: none -> 4.06 us  [the longest x1 2.25 us: body(): later.append(lax.ppermute(later[-1], 'grp', down_2))]
    ppermute x0 -> x3, waiting for transfers between devices: none -> 3.94 us  [the longest x2 3.94 us: body(): earlier.append(lax.ppermute(earlier[-1], 'grp', up))]
    all_gather x1, blocking collectives: 10.7 us -> 8.2 us  [body(): group_sources = lax.all_gather(source, 'nbr', axis=0, tiled=True)]
    psum x1, blocking collectives: 23.6 us -> 25.5 us  [body(): lax.psum(jnp.dot(onehot.T, lifted, precision=lax.Precision.HIGHEST, prefe...]
    unnamed x16 -> x23, local copies, waits for them, and re-layouts: 3.21 us -> 3.28 us
  transfers between devices with their start and end apart: 0 -> 3, of which waited for: 0 -> 1; matrix products, arithmetic and copies ran while one was open for 0% -> 36% of each run, Pallas kernels for 0% -> 0%
where the time goes in v1:
time: 94.5 us; the launch traced here: 94.1 us
  blocking collectives  42.8 us (45%)
  local copies, waits for them, and re-layouts  30.2 us (32%)
  matrix products  9.24 us (10%)
  starting transfers between devices  4.06 us (4%)
  waiting for transfers between devices  3.94 us (4%)
  other arithmetic  2.25 us (2%)
  between operations  1.62 us (2%)
    psum x1, blocking collectives, body(): lax.psum(jnp.dot(onehot.T, lifted, precision=lax.Precision.HIGHEST, prefe...  25.5 us
    reshape x2, local copies, waits for them, and re-layouts, couple(): picked.reshape(slots, width, K, R)  9.44 us
    all_gather x1, blocking collectives, body(): group_local = lax.all_gather(coarse_local, 'nbr', axis=0, tiled=True)  9.08 us
    dot_general x2, matrix products, couple(): jnp.einsum('tjik,tjkr->tjir', blocks.reshape(slots, width, K, K), picked....  8.56 us
    all_gather x1, blocking collectives, body(): group_sources = lax.all_gather(source, 'nbr', axis=0, tiled=True)  8.2 us
    reshape x1, local copies, waits for them, and re-layouts, couple(): blocks.reshape(slots, width, K, K)  6.6 us
    gather x2, local copies, waits for them, and re-layouts, body(): group_sources[local_source]  4.39 us
    ppermute x2, waiting for transfers between devices, body(): earlier.append(lax.ppermute(earlier[-1], 'grp', up))  3.94 us
  transfers between devices with their start and end apart: 3, of which 1 were waited for; matrix products, arithmetic and copies ran while one was open for 36% of the time, Pallas kernels for 0%

profile of v1, /device:TPU:0, one launch (start us, length us, event | category | flops | bytes accessed | tf_op | source)
XLA Modules:
  0.0 94.1 jit_solution(3253614619466297413)
XLA Ops:
  0.7 0.8 broadcast_select_fusion
  1.5 0.1 reshape.78
  1.6 0.8 reshape.79
  2.4 0.2 convolution_bitcast_fusion
  2.6 0.1 copy.47
  2.8 0.1 reshape.80
  2.9 0.7 compare_select_fusion.1
  3.5 0.3 fusion.4
  3.8 25.5 %psum.7 = bf16[8,1024]{1,0:T(8,128)(2,1)S(1)} all-reduce(f32[8,1024]{1,0:T(8,128)S(1)} %fusion.4), channel_id=1, replica_groups=mesh['grp'=4,'nbr'=8] {'nbr'}, use_global_device_ids=true, to_apply=%region_1.2 | all-reduce | flops 8192 | bytes 49152 | tf_op jit(solution)/shard_map/psum | solution.py:54
  29.3 1.6 %collective-permute-start = (bf16[8,1024]{1,0:T(8,128)(2,1)S(1)}, bf16[8,1024]{1,0:T(8,128)(2,1)S(1)}, u32[]{:S(2)}, u32[]{:S(2)}) collective-permute-start(bf16[8,1024]{1,0:T(8,128)(2,1)S(1)} %psum.7), channel_id=1, source_target_pairs={{0,8},{8,16},{16,24},{24,0},{1,9},{9,17},{17,25},{25,1},{2,10},{10... | collective-permute-start | bytes 49160 | tf_op jit(solution)/shard_map/ppermute | solution.py:66
  30.9 2.2 %collective-permute-start.2 = (bf16[8,1024]{1,0:T(8,128)(2,1)S(1)}, bf16[8,1024]{1,0:T(8,128)(2,1)S(1)}, u32[]{:S(2)}, u32[]{:S(2)}) collective-permute-start(bf16[8,1024]{1,0:T(8,128)(2,1)S(1)} %psum.7), channel_id=1, source_target_pairs={{0,24},{8,0},{16,8},{24,16},{1,25},{9,1},{17,9},{25,17},{2,26},{10... | collective-permute-start | bytes 49160 | tf_op jit(solution)/shard_map/ppermute | solution.py:68
  33.1 8.2 %all_gather.6 = bf16[64,1024]{1,0:T(8,128)(2,1)S(1)} all-gather(bf16[8,1024]{1,0:T(8,128)(2,1)S(1)} %broadcast_select_fusion), channel_id=1, replica_groups=mesh['grp'=4,'nbr'=8] {'nbr'}, dimensions={0}, use_global_device_ids=true | all-gather | bytes 147456 | tf_op jit(solution)/shard_map/all_gather | solution.py:71
  41.3 0.7 compare_select_fusion
  42.0 0.1 reshape.87
  42.1 2.8 %gather_fusion = bf16[768,1024]{1,0:T(8,128)(2,1)S(1)} fusion(bf16[64,1024]{1,0:T(8,128)(2,1)S(1)} %all_gather.6, s32[1024]{0:T(1024)S(1)} %pad_clamp_fusion.2), kind=kCustom, calls=%fused_computation | custom fusion | bytes 3148800 | tf_op jit(solution)/shard_map/gather | solution.py:76
  44.9 1.6 %copy.42 = bf16[768,1024]{0,1:T(8,128)(2,1)} copy(bf16[768,1024]{1,0:T(8,128)(2,1)S(1)} %gather_fusion) | data formatting | bytes 3145728 | tf_op jit(solution)/shard_map/gather | solution.py:76
  46.5 3.7 %reshape.76 = bf16[8,96,32,32]{1,0,3,2:T(8,128)(2,1)S(1)} reshape(bf16[768,1024]{0,1:T(8,128)(2,1)} %copy.42) | data formatting | bytes 3145728 | tf_op jit(solution)/shard_map/reshape | solution.py:16
  50.3 5.7 %copy.44 = bf16[8,96,32,32]{2,3,1,0:T(8,128)(2,1)} copy(bf16[8,96,32,32]{1,0,3,2:T(8,128)(2,1)S(1)} %reshape.76) | data formatting | bytes 3145728 | tf_op jit(solution)/shard_map/reshape | solution.py:16
  56.0 0.0 copy-start.4
  56.0 0.0 copy-start.2
  56.0 0.0 copy-start.3
  56.0 0.0 copy-start.5
  56.0 3.0 %copy.43 = bf16[8,96,1024]{1,2,0:T(8,128)(2,1)S(1)} copy(bf16[8,96,1024]{2,1,0:T(8,128)(2,1)} %param.19) | data formatting | bytes 3145728 | tf_op args[6]
  59.0 6.6 %copy.45 = bf16[8,96,32,32]{3,2,1,0:T(8,128)(2,1)} copy(bf16[8,96,32,32]{1,3,2,0:T(8,128)(2,1)S(1)} %bitcast.32) | data formatting | bytes 3145728 | tf_op jit(solution)/shard_map/reshape | solution.py:15
  65.6 0.0 copy-done.4
  66.2 0.0 copy-done.2
  66.2 0.0 copy-done.3
  66.2 0.1 fusion.3
  66.3 0.0 copy-done.5
  66.3 0.0 copy-start
  66.3 0.0 copy-start.1
  66.3 8.0 %multiply_reduce_fusion = f32[8,32,32]{2,1,0:T(8,128)S(1)} fusion(f32[8,96]{1,0:T(8,128)S(1)} %fusion.3, bf16[8,96,32,32]{2,3,1,0:T(8,128)(2,1)} %copy.44, bf16[8,96,32,32]{3,2,1,0:T(8,128)(2,1)} %copy.45), kind=kOutput, calls=%fused_computation.3 | convolution fusion | flops 51896320 | bytes 3181568 | tf_op jit(solution)/shard_map/tjik,tjkr->tjir/dot_general | solution.py:13
  74.4 0.0 collective-permute-done
  74.4 0.2 collective-permute-start.1
  74.7 0.0 copy-done
  74.7 0.2 copy.49
  74.9 1.2 %copy.51 = bf16[96,32,32]{2,1,0:T(8,128)(2,1)S(1)} copy(bf16[96,32,32]{0,2,1:T(8,128)(2,1)S(1)} %bitcast.35) | data formatting | bytes 393216 | tf_op jit(solution)/shard_map/reshape
  76.1 0.0 copy-done.1
  76.1 0.1 reshape.84
  76.2 3.9 %collective-permute-done.1 = bf16[8,1024]{1,0:T(8,128)(2,1)S(1)} collective-permute-done((bf16[8,1024]{1,0:T(8,128)(2,1)S(1)}, bf16[8,1024]{1,0:T(8,128)(2,1)S(1)}, u32[]{:S(2)}, u32[]{:S(2)}) %collective-permute-start.1) | collective-permute-done | bytes 16416 | tf_op jit(solution)/shard_map/ppermute | solution.py:66
  80.2 0.0 collective-permute-done.2
  80.3 0.8 gather_fusion.1
  81.0 0.2 copy.48
  81.2 1.3 %copy.50 = bf16[96,32,32]{1,2,0:T(8,128)(2,1)S(1)} copy(bf16[96,32,32]{0,2,1:T(8,128)(2,1)S(1)} %bitcast.34) | data formatting | bytes 393216 | tf_op jit(solution)/shard_map/reshape.1
  82.5 0.5 multiply_reduce_fusion.1
  83.1 0.1 copy.52
  83.2 0.1 reshape.115
  83.2 9.1 %all-gather = bf16[8,1,1024]{2,1,0:T(2,128)(2,1)S(1)} all-gather(bf16[1,1,1024]{2,1,0:T(2,128)(2,1)S(1)} %reshape.115), channel_id=1, replica_groups=mesh['grp'=4,'nbr'=8] {'nbr'}, dimensions={0}, use_global_device_ids=true | all-gather | bytes 18432 | tf_op jit(solution)/shard_map/all_gather | solution.py:77
  92.3 0.6 gather_fusion.2
  92.9 0.1 reshape.83
  93.0 0.2 fusion.2
  93.3 0.1 copy.54
  93.4 0.7 convert_element_type.36
  (16 shorter events, 0.1 us)
Async XLA Ops:
  29.3 45.1 %collective-permute-start = (bf16[8,1024]{1,0:T(8,128)(2,1)S(1)}, bf16[8,1024]{1,0:T(8,128)(2,1)S(1)}, u32[]{:S(2)}, u32[]{:S(2)}) collective-permute-start(bf16[8,1024]{1,0:T(8,128)(2,1)S(1)} %psum.7), channel_id=1, source_target_pairs={{0,8},{8,16},{16,24},{24,0},{1,9},{9,17},{17,25},{25,1},{2,10},{10... | collective-permute-start | bytes 49160 | tf_op jit(solution)/shard_map/ppermute | solution.py:66
  30.9 49.3 %collective-permute-start.2 = (bf16[8,1024]{1,0:T(8,128)(2,1)S(1)}, bf16[8,1024]{1,0:T(8,128)(2,1)S(1)}, u32[]{:S(2)}, u32[]{:S(2)}) collective-permute-start(bf16[8,1024]{1,0:T(8,128)(2,1)S(1)} %psum.7), channel_id=1, source_target_pairs={{0,24},{8,0},{16,8},{24,16},{1,25},{9,1},{17,9},{25,17},{2,26},{10... | collective-permute-start | bytes 49160 | tf_op jit(solution)/shard_map/ppermute | solution.py:68
  56.0 9.6 %copy-start.4 = (s32[1,96]{1,0:T(1,128)S(1)}, s32[1,96]{1,0:T(1,128)}, u32[]{:S(2)}) copy-start(s32[1,96]{1,0:T(1,128)} %param.21) | copy-start | bytes 1156
  56.0 10.3 %copy-start.2 = (f32[8,96]{1,0:T(8,128)S(1)}, f32[8,96]{1,0:T(8,128)}, u32[]{:S(2)}) copy-start(f32[8,96]{1,0:T(8,128)} %param.20) | copy-start | bytes 9220
  56.0 10.3 %copy-start.3 = (s32[8]{0:T(128)S(1)}, s32[8]{0:T(128)}, u32[]{:S(2)}) copy-start(s32[8]{0:T(128)} %param.18) | copy-start | bytes 100
  56.0 10.3 %copy-start.5 = (f32[1,96]{1,0:T(1,128)S(1)}, f32[1,96]{1,0:T(1,128)}, u32[]{:S(2)}) copy-start(f32[1,96]{1,0:T(1,128)} %param.24) | copy-start | bytes 1156
  66.3 8.4 %copy-start = (bf16[1,96,1024]{2,1,0:T(8,128)(2,1)S(1)}, bf16[1,96,1024]{2,1,0:T(8,128)(2,1)}, u32[]{:S(2)}) copy-start(bf16[1,96,1024]{2,1,0:T(8,128)(2,1)} %param.23) | copy-start | bytes 589828
  66.3 9.8 %copy-start.1 = (bf16[8,1024]{1,0:T(8,128)(2,1)S(1)}, bf16[8,1024]{1,0:T(8,128)(2,1)}, u32[]{:S(2)}) copy-start(bf16[8,1024]{1,0:T(8,128)(2,1)} %param.25) | copy-start | bytes 49156
  74.4 5.8 %collective-permute-start.1 = (bf16[8,1024]{1,0:T(8,128)(2,1)S(1)}, bf16[8,1024]{1,0:T(8,128)(2,1)S(1)}, u32[]{:S(2)}, u32[]{:S(2)}) collective-permute-start(bf16[8,1024]{1,0:T(8,128)(2,1)S(1)} %collective-permute-done), channel_id=1, source_target_pairs={{0,8},{8,16},{16,24},{24,0},{1,9},{9,17},{17,25},{25,1},{2,10},{10... | collective-permute-start | bytes 49160 | tf_op jit(solution)/shard_map/ppermute | solution.py:66
